TPU v7x, 256 devices: a whole 4x4x8 slice. The times are simulated.
256 devices in a mesh: eig: 16 (over x, z_hi, core), store: 16 (over z_lo, y).
Axes of the slice: x: 4, y: 4, z: 8 (z_hi: 2, z_lo: 4; z = z_hi * 4 + z_lo), core: 2. Of those that a mesh axis runs over, the one named last changes fastest.
Arguments:
- acts: bfloat16 [2048, 8192], P('store'), may hold values from -6 to 6
- basis: bfloat16 [8192, 8192], P('store', 'eig'), may hold values from -0.0625 to 0.0625
- eigvals: float32 [64, 8192], P(None, 'eig'), may hold values from 0.5 to 8
- projection: bfloat16 [8192, 64], P('eig'), may hold values from -0.0625 to 0.0625
- out_factor: float32 [2048, 64], P('store', 'eig'), may hold values from -6 to 6
- store: bfloat16 [32768, 4096], P('store', 'eig'), may hold values from -0.09375 to 0.09375
Outputs:
- scores: float32 [2048, 32768], P(None, ('store', 'eig'))
All inputs are finite; a program needn't handle non-finite values.
Results may differ from a plain program's by a relative error of at most 0.0041.
Values may be sent and summed in bfloat16 or wider, within the bound.
A program may use at most 64 MiB of HBM per device.

v0:
```python
import jax
import jax.numpy as jnp
from jax import lax
from jax.sharding import PartitionSpec as P

K_OUT = 64
K_IN = 64
damping = 0.1


def joined_along(blocks, dim):
    blocks = jnp.moveaxis(blocks, 0, dim)
    shape = blocks.shape
    return blocks.reshape(*shape[:dim], shape[dim] * shape[dim + 1], *shape[dim + 2 :])


def from_everyone(shard, axis):
    copies = jnp.broadcast_to(shard, (lax.axis_size(axis), *shard.shape))
    return lax.all_to_all(copies, axis, split_axis=0, concat_axis=0, tiled=True)


def gathered_copies(shard, axis, dim):
    return joined_along(from_everyone(shard, axis), dim)


def body(acts, basis, eigvals, projection, out_factor, store):
    queries = acts.shape[0]
    columns = basis.shape[1]
    rotated = jnp.dot(
        acts, lax.all_gather(basis, "store", axis=0, tiled=True), preferred_element_type=jnp.float32
    )
    inverse = 1.0 / (eigvals + damping)
    scaled = (rotated[:, None, :] * inverse[None, :, :]).astype(jnp.bfloat16)
    partial_value = jnp.dot(
        scaled.reshape(queries * K_OUT, columns), projection, preferred_element_type=jnp.float32
    )
    partial_value = partial_value.reshape(queries, K_OUT * K_IN)
    summed = lax.psum_scatter(partial_value, "eig", scatter_dimension=1, tiled=True)
    kept = out_factor.shape[1]
    features = (summed.reshape(queries, kept, K_IN) * out_factor[:, :, None]).reshape(
        queries, kept * K_IN
    )
    features = features.astype(jnp.bfloat16)
    partial_scores = jnp.einsum(
        "qf,rf->qr",
        gathered_copies(features, "store", 0),
        store,
        preferred_element_type=jnp.float32,
    )
    return lax.psum_scatter(partial_scores, "eig", scatter_dimension=1, tiled=True)


def solution(mesh):
    placed = (
        P("store", None),
        P("store", "eig"),
        P(None, "eig"),
        P("eig", None),
        P("store", "eig"),
        P("store", "eig"),
    )
    return jax.shard_map(
        body, mesh=mesh, in_specs=placed, out_specs=P(None, ("store", "eig")), check_vma=False
    )
```

profile of v0, /device:TPU:1, one launch (start us, length us, event | category | flops | bytes accessed | tf_op | source)
XLA Modules:
  0.0 479.9 jit_solution(4561740160038415110)
XLA Ops:
  6.5 0.0 copy-start
  6.5 0.0 all-gather.2.cloned.1.call-start
  6.5 0.7 all-gather.2.cloned.1.call-update
  7.3 0.0 reduce-scatter.3.cloned.1.call-start
  7.3 0.9 add_divide_fusion
  8.2 107.2 %all-gather.2.cloned.1.call-done = bf16[8192,512]{1,0:T(8,128)(2,1)} async-done(((bf16[512,512]{1,0:T(8,128)(2,1)}), bf16[8192,512]{1,0:T(8,128)(2,1)}) %all-gather.2.cloned.1.call-update) | async-done | bytes 8388624 | tf_op jit(solution)/shard_map/all_gather | solution.py:30
  115.5 0.0 copy-done
  115.5 4.6 fusion
  120.1 0.0 copy-start.2
  120.1 3.4 multiply_convert_fusion
  123.5 0.0 copy-done.2
  123.5 4.3 fusion.1
  127.8 0.0 copy-start.3
  127.8 0.0 copy-start.1
  127.8 4.8 %reshape.17 = f32[128,4096]{1,0:T(8,128)} reshape(f32[8192,64]{1,0:T(8,128)} %fusion.1) | data formatting | bytes 4194304 | tf_op jit(solution)/shard_map/reshape | solution.py:37
  132.6 0.0 reduce-scatter.3.cloned.1.call-update
  132.6 0.0 reduce-scatter.5.cloned.1.call-start
  132.7 0.0 copy-done.3
  132.7 0.1 copy.9
  132.8 82.8 %reduce-scatter.3.cloned.1.call-done = f32[128,256]{1,0:T(8,128)} async-done(((f32[128,4096]{1,0:T(8,128)}), f32[128,256]{1,0:T(8,128)}) %reduce-scatter.3.cloned.1.call-update) | async-done | bytes 131088 | tf_op jit(solution)/shard_map/reduce_scatter | solution.py:38
  215.6 0.9 multiply_convert_fusion.1
  216.5 0.1 broadcast_in_dim.2
  216.6 28.1 %all_to_all.5 = bf16[16,128,256]{2,1,0:T(8,128)(2,1)S(1)} all-to-all(bf16[16,128,256]{2,1,0:T(8,128)(2,1)S(1)} %broadcast_in_dim.2), channel_id=1, replica_groups=mesh['eig'=16,'store'=16] {'store'}, dimensions={0} | all-to-all | bytes 2097152 | tf_op jit(solution)/shard_map/all_to_all | solution.py:19
  244.7 0.0 copy-done.1
  244.7 8.1 %fusion.2 = f32[2048,2048]{1,0:T(8,128)} fusion(bf16[2048,256]{1,0:T(8,128)(2,1)S(1)} %bitcast.10, bf16[2048,256]{1,0:T(8,128)(2,1)S(1)} %copy-done.1), kind=kOutput, calls=%fused_computation.5 | convolution fusion | flops 2147483648 | bytes 18874368 | tf_op jit(solution)/shard_map/qf,rf->qr/dot_general | solution.py:44
  252.8 0.0 reduce-scatter.5.cloned.1.call-update
  252.8 220.6 %reduce-scatter.5.cloned.1.call-done = f32[2048,128]{1,0:T(8,128)} async-done(((f32[2048,2048]{1,0:T(8,128)}), f32[2048,128]{1,0:T(8,128)}) %reduce-scatter.5.cloned.1.call-update) | async-done | bytes 1048592 | tf_op jit(solution)/shard_map/reduce_scatter | solution.py:50
  (1 shorter events, 0.0 us)
Async XLA Ops:
  6.5 108.9 %copy-start = (bf16[128,8192]{1,0:T(8,128)(2,1)S(1)}, bf16[128,8192]{1,0:T(8,128)(2,1)}, u32[]{:S(2)}) copy-start(bf16[128,8192]{1,0:T(8,128)(2,1)} %param.6) | copy-start | bytes 6291460
  6.5 108.9 %all-gather.2.cloned.1.call-start = ((), (), s32[]{:S(2)}) async-start(), calls=%async_computation.3 | async-start | bytes 8912896 | tf_op jit(solution)/shard_map/all_gather | solution.py:30
  7.3 208.3 %reduce-scatter.3.cloned.1.call-start = ((), (), s32[]{:S(2)}) async-start(), calls=%async_computation.4 | async-start | bytes 2228224 | tf_op jit(solution)/shard_map/reduce_scatter | solution.py:38
  120.1 3.4 copy-start.2
  127.8 4.9 %copy-start.3 = (f32[128,4]{0,1:T(4,128)S(1)}, f32[128,4]{0,1:T(4,128)}, u32[]{:S(2)}) copy-start(f32[128,4]{0,1:T(4,128)} %param.10) | copy-start | bytes 6148
  127.8 116.9 %copy-start.1 = (bf16[2048,256]{1,0:T(8,128)(2,1)S(1)}, bf16[2048,256]{1,0:T(8,128)(2,1)}, u32[]{:S(2)}) copy-start(bf16[2048,256]{1,0:T(8,128)(2,1)} %param.11) | copy-start | bytes 3145732
  132.6 340.8 %reduce-scatter.5.cloned.1.call-start = ((), (), s32[]{:S(2)}) async-start(), calls=%async_computation.5 | async-start | bytes 17825792 | tf_op jit(solution)/shard_map/reduce_scatter | solution.py:50
Sparse Core Ops, SparseCore 0:
  9.1 106.2 all-gather.1
  132.8 82.7 reduce-scatter.2
  252.9 220.4 reduce-scatter.4
where the time goes:
time: 480 us
  waiting for transfers between devices  411 us (86%)
  blocking collectives  28.1 us (6%)
  matrix products  17 us (4%)
  between operations  13.2 us (3%)
  other arithmetic  5.2 us (1%)
  local copies, waits for them, and re-layouts  5.06 us (1%)
    reduce_scatter x1, waiting for transfers between devices, body(): lax.psum_scatter(partial_scores, 'eig', scatter_dimension=1, tiled=True)  221 us
    all_gather x1, waiting for transfers between devices, body(): lax.all_gather(basis, 'store', axis=0, tiled=True)  107 us
    reduce_scatter x1, waiting for transfers between devices, body(): lax.psum_scatter(partial_value, 'eig', scatter_dimension=1, tiled=True)  82.8 us
    all_to_all x1, blocking collectives, from_everyone(): return lax.all_to_all(copies, axis, split_axis=0, concat_axis=0, tiled=True)  28.1 us
  transfers between devices with their start and end apart: 3, of which 3 were waited for; matrix products, arithmetic and copies ran while one was open for 0% of the time, Pallas kernels for 0%

commit v1 on v0

--- a/solution.py
+++ b/solution.py
@@ -27,7 +27,11 @@
     queries = acts.shape[0]
     columns = basis.shape[1]
     rotated = jnp.dot(
-        acts, lax.all_gather(basis, "store", axis=0, tiled=True), preferred_element_type=jnp.float32
+        acts,
+        jnp.concatenate(
+            lax.all_to_all(jnp.stack([basis] * lax.axis_size("store")), "store", 0, 0), axis=0
+        ),
+        preferred_element_type=jnp.float32,
     )
     inverse = 1.0 / (eigvals + damping)
     scaled = (rotated[:, None, :] * inverse[None, :, :]).astype(jnp.bfloat16)

time: 480 us -> 573 us (1.19)
  waiting for transfers between devices: 411 us -> 490 us
  starting transfers between devices: 0.08 us -> 9.45 us
    all_to_all x0 -> x1, waiting for transfers between devices: none -> 151 us  [body(): lax.all_to_all(jnp.stack([basis] * lax.axis_size('store')), 'store', 0, 0)]
    all_gather x1 -> x0, waiting for transfers between devices: 107 us -> none  [body(): lax.all_gather(basis, 'store', axis=0, tiled=True)]
    reduce_scatter x1, waiting for transfers between devices: 82.8 us -> 118 us  [body(): lax.psum_scatter(partial_value, 'eig', scatter_dimension=1, tiled=True)]
    all_to_all x0 -> x1, starting transfers between devices: none -> 9.37 us  [body(): lax.all_to_all(jnp.stack([basis] * lax.axis_size('store')), 'store', 0, 0)]
where the time goes in v1:
time: 573 us; the launch traced here: 572 us
  waiting for transfers between devices  490 us (86%)
  blocking collectives  28.1 us (5%)
  matrix products  17 us (3%)
  between operations  13.5 us (2%)
  local copies, waits for them, and re-layouts  10.3 us (2%)
  starting transfers between devices  9.45 us (2%)
    reduce_scatter x1, waiting for transfers between devices, body(): lax.psum_scatter(partial_scores, 'eig', scatter_dimension=1, tiled=True)  220 us
    all_to_all x1, waiting for transfers between devices, body(): lax.all_to_all(jnp.stack([basis] * lax.axis_size('store')), 'store', 0, 0)  151 us
    reduce_scatter x1, waiting for transfers between devices, body(): lax.psum_scatter(partial_value, 'eig', scatter_dimension=1, tiled=True)  118 us
    all_to_all x1, blocking collectives, from_everyone(): return lax.all_to_all(copies, axis, split_axis=0, concat_axis=0, tiled=True)  28.1 us
  transfers between devices with their start and end apart: 3, of which 3 were waited for; matrix products, arithmetic and copies ran while one was open for 0% of the time, Pallas kernels for 0%

profile of v1, /device:TPU:1, one launch (start us, length us, event | category | flops | bytes accessed | tf_op | source)
XLA Modules:
  0.0 572.4 jit_solution(16063353743082047149)
XLA Ops:
  6.5 0.0 copy-start
  6.5 5.2 stack.2
  11.8 0.0 copy-start.2
  11.8 9.4 %all-to-all-start = ((bf16[16,512,512]{2,1,0:T(8,128)(2,1)}), bf16[16,512,512]{2,1,0:T(8,128)(2,1)}, u32[]{:S(2)}, u32[]{:S(2)}) async-start(bf16[16,512,512]{2,1,0:T(8,128)(2,1)} %stack.2), calls=%async_computation | async-start | bytes 16777216 | tf_op jit(solution)/shard_map/all_to_all | solution.py:32
  21.1 0.0 reduce-scatter.3.cloned.1.call-start
  21.2 0.0 copy-done.2
  21.2 151.2 %all-to-all-done = bf16[16,512,512]{2,1,0:T(8,128)(2,1)} async-done(((bf16[16,512,512]{2,1,0:T(8,128)(2,1)}), bf16[16,512,512]{2,1,0:T(8,128)(2,1)}, u32[]{:S(2)}, u32[]{:S(2)}) %all-to-all-start) | async-done | bytes 8388640 | tf_op jit(solution)/shard_map/all_to_all | solution.py:32
  172.4 0.0 copy-done
  172.4 4.6 fusion
  177.0 0.0 copy-start.3
  177.0 3.4 multiply_convert_fusion
  180.4 0.0 copy-done.3
  180.4 4.3 fusion.1
  184.7 0.0 copy-start.4
  184.7 0.0 copy-start.1
  184.7 4.8 reshape.23
  189.5 0.0 reduce-scatter.3.cloned.1.call-update
  189.6 0.0 reduce-scatter.5.cloned.1.call-start
  189.6 0.0 copy-done.4
  189.6 0.1 copy.9
  189.7 118.1 %reduce-scatter.3.cloned.1.call-done = f32[128,256]{1,0:T(8,128)} async-done(((f32[128,4096]{1,0:T(8,128)}), f32[128,256]{1,0:T(8,128)}) %reduce-scatter.3.cloned.1.call-update) | async-done | bytes 131088 | tf_op jit(solution)/shard_map/reduce_scatter | solution.py:42
  307.9 0.9 multiply_convert_fusion.1
  308.8 0.1 broadcast_in_dim.2
  308.9 28.1 %all_to_all.10 = bf16[16,128,256]{2,1,0:T(8,128)(2,1)S(1)} all-to-all(bf16[16,128,256]{2,1,0:T(8,128)(2,1)S(1)} %broadcast_in_dim.2), channel_id=1, replica_groups=mesh['eig'=16,'store'=16] {'store'}, dimensions={0} | all-to-all | bytes 2097152 | tf_op jit(solution)/shard_map/all_to_all | solution.py:19
  337.0 0.0 copy-done.1
  337.0 8.1 %fusion.2 = f32[2048,2048]{1,0:T(8,128)} fusion(bf16[2048,256]{1,0:T(8,128)(2,1)S(1)} %bitcast.11, bf16[2048,256]{1,0:T(8,128)(2,1)S(1)} %copy-done.1), kind=kOutput, calls=%fused_computation.5 | convolution fusion | flops 2147483648 | bytes 18874368 | tf_op jit(solution)/shard_map/qf,rf->qr/dot_general | solution.py:48
  345.1 0.0 reduce-scatter.5.cloned.1.call-update
  345.1 220.5 %reduce-scatter.5.cloned.1.call-done = f32[2048,128]{1,0:T(8,128)} async-done(((f32[2048,2048]{1,0:T(8,128)}), f32[2048,128]{1,0:T(8,128)}) %reduce-scatter.5.cloned.1.call-update) | async-done | bytes 1048592 | tf_op jit(solution)/shard_map/reduce_scatter | solution.py:54
  (2 shorter events, 0.0 us)
Async XLA Ops:
  6.5 165.9 %copy-start = (bf16[128,8192]{1,0:T(8,128)(2,1)S(1)}, bf16[128,8192]{1,0:T(8,128)(2,1)}, u32[]{:S(2)}) copy-start(bf16[128,8192]{1,0:T(8,128)(2,1)} %param.6) | copy-start | bytes 6291460
  11.8 9.4 %copy-start.2 = (f32[64,512]{1,0:T(8,128)S(1)}, f32[64,512]{1,0:T(8,128)}, u32[]{:S(2)}) copy-start(f32[64,512]{1,0:T(8,128)} %param.8) | copy-start | bytes 393220
  11.8 160.6 %all-to-all-start = ((bf16[16,512,512]{2,1,0:T(8,128)(2,1)}), bf16[16,512,512]{2,1,0:T(8,128)(2,1)}, u32[]{:S(2)}, u32[]{:S(2)}) async-start(bf16[16,512,512]{2,1,0:T(8,128)(2,1)} %stack.2), calls=%async_computation | async-start | bytes 16777216 | tf_op jit(solution)/shard_map/all_to_all | solution.py:32
  21.1 286.7 %reduce-scatter.3.cloned.1.call-start = ((), (), s32[]{:S(2)}) async-start(), calls=%async_computation.4 | async-start | bytes 2228224 | tf_op jit(solution)/shard_map/reduce_scatter | solution.py:42
  177.0 3.4 copy-start.3
  184.7 4.9 copy-start.4
  184.7 152.3 %copy-start.1 = (bf16[2048,256]{1,0:T(8,128)(2,1)S(1)}, bf16[2048,256]{1,0:T(8,128)(2,1)}, u32[]{:S(2)}) copy-start(bf16[2048,256]{1,0:T(8,128)(2,1)} %param.11) | copy-start | bytes 3145732
  189.6 376.0 %reduce-scatter.5.cloned.1.call-start = ((), (), s32[]{:S(2)}) async-start(), calls=%async_computation.5 | async-start | bytes 17825792 | tf_op jit(solution)/shard_map/reduce_scatter | solution.py:54
Sparse Core Ops, SparseCore 0:
  189.7 118.1 reduce-scatter.2
  345.2 220.3 reduce-scatter.4
